TPU v7x, 32 devices: a whole 2x2x4 slice. The times are simulated.
32 devices in a mesh: ctx: 8 (over z, x), exp: 4 (over y, core).
Axes of the slice: x: 2, y: 2, z: 4, core: 2. Of those that a mesh axis runs over, the one named last changes fastest.
Arguments:
- stored: bfloat16 [4, 4096, 2048], P(None, 'ctx'), may hold values from -50 to 50
- depth_weights: float32 [4], replicated, may hold values from 0.2 to 1
- attn_gain: float32 [2048], replicated, may hold values from 0.5 to 1.5
- qkv_proj: bfloat16 [2048, 3, 16, 128], P(None, None, 'exp'), may hold values from -0.125 to 0.125
- q_gain: float32 [16, 128], P('exp'), may hold values from 1 to 2.5
- k_gain: float32 [16, 128], P('exp'), may hold values from 1 to 2.5
- out_proj: bfloat16 [2048, 2048], P('exp'), may hold values from -0.5 to 0.5
- moe_gain: float32 [2048], replicated, may hold values from 0.5 to 1.5
- router: bfloat16 [2048, 16], replicated, may hold values from -0.125 to 0.125
- gate_proj: bfloat16 [2048, 22528], P(None, ('ctx', 'exp')), may hold values from -0.125 to 0.125
- up_proj: bfloat16 [2048, 22528], P(None, ('ctx', 'exp')), may hold values from -0.125 to 0.125
- down_proj: bfloat16 [22528, 2048], P(('ctx', 'exp')), may hold values from -0.15625 to 0.15625
- expert_ids: int32 [4096, 6], P(('ctx', 'exp')), may hold values from 0 to 15, all different within a row; in each aligned block of 128 rows (0 to 127, 128 to 255, ...) at most 64 rows name the same one
- block_pattern: int32 [16, 64, 8], replicated, may hold values from -1 to 63, as said below
Outputs:
- layer_out: bfloat16 [4096, 2048], P(('ctx', 'exp'))
Inputs may be any that keep to these rules, and one draw needn't show every extreme that they name: `expert_ids`: each row names 6 different experts; among the 128 rows of one device no expert is named by more than 64 rows, and some device reaches 64. Entry 0 of block_pattern[h, b] is b; the other 7 entries are distinct blocks before b, or -1 where fewer blocks precede b.
All inputs are finite; a program needn't handle non-finite values.
Results may differ from a plain program's by a relative error of at most 0.015.
Values may be sent and summed in bfloat16 or wider, within the bound.
A program may use at most 128 MiB of HBM per device.

v0:
```python
import jax
import jax.numpy as jnp
from jax import lax
from jax.sharding import PartitionSpec as P

BLK = 64


EPSILON = 1e-06


def partner(value, axis, distance):
    mask = 2**distance
    pairs = [(source, source ^ mask) for source in range(lax.axis_size(axis))]
    return lax.ppermute(value, axis, pairs)


def rms_scale(values, gain_vec):
    mean_sq = jnp.mean(values * values, axis=-1, keepdims=True)
    return values * lax.rsqrt(mean_sq + EPSILON) * gain_vec


def attend_blocks(q_blocks, key_blocks, value_blocks, pattern_rows, block_ids):
    listed = pattern_rows >= 0
    safe_ids = jnp.maximum(pattern_rows, 0)
    key_sel = jnp.take(key_blocks, safe_ids, axis=0)
    value_sel = jnp.take(value_blocks, safe_ids, axis=0)
    score_scale = q_blocks.shape[-1] ** (-0.5)
    scores = (
        jnp.einsum("nid,nkjd->nikj", q_blocks, key_sel, preferred_element_type=jnp.float32)
        * score_scale
    )
    diagonal = pattern_rows == block_ids[:, None]
    row_pos = lax.broadcasted_iota(jnp.int32, scores.shape, 1)
    col_pos = lax.broadcasted_iota(jnp.int32, scores.shape, 3)
    visible = listed[:, None, :, None] & (~diagonal[:, None, :, None] | (col_pos <= row_pos))
    weights = jnp.where(visible, jnp.exp(scores), jnp.float32(0.0))
    totals = jnp.sum(weights, axis=(2, 3))
    summed = jnp.einsum(
        "nikj,nkjd->nid",
        weights.astype(jnp.bfloat16),
        value_sel,
        preferred_element_type=jnp.float32,
    )
    return (summed / totals[..., None]).astype(jnp.bfloat16)


def body(
    stored,
    depth_weights,
    attn_gain,
    qkv_proj,
    q_gain,
    k_gain,
    out_proj,
    moe_gain,
    router,
    gate_proj,
    up_proj,
    down_proj,
    expert_ids,
    block_pattern,
):
    ctx_count = lax.axis_size("ctx")
    exp_count = lax.axis_size("exp")
    ctx_index = lax.axis_index("ctx")
    exp_index = lax.axis_index("exp")
    depth_count, shard_len, feat_width = stored.shape
    blended = depth_weights[0] * stored[0].astype(jnp.float32)
    for depth_step in range(1, depth_count):
        blended = blended + depth_weights[depth_step] * stored[depth_step].astype(jnp.float32)
    inputs = blended.astype(jnp.bfloat16)
    normed = rms_scale(inputs.astype(jnp.float32), attn_gain).astype(jnp.bfloat16)
    projected = jnp.einsum("td,dche->chte", normed, qkv_proj, preferred_element_type=jnp.float32)
    head_group = projected.shape[1]
    head_dim = projected.shape[3]
    query_parts = ctx_count // head_group
    piece_len = shard_len // query_parts
    queries = rms_scale(projected[0], q_gain[:, None, :]).astype(jnp.bfloat16)
    key_heads = rms_scale(projected[1], k_gain[:, None, :]).astype(jnp.bfloat16)
    value_heads = projected[2].astype(jnp.bfloat16)
    query_send = queries.reshape(head_group * query_parts, piece_len, head_dim)
    key_value = jnp.concatenate([key_heads, value_heads], axis=2)
    pair_send = jnp.repeat(key_value, query_parts, axis=0)
    query_all, pair_all = (
        lax.all_to_all(query_send, "ctx", split_axis=0, concat_axis=1, tiled=True),
        lax.all_to_all(pair_send, "ctx", split_axis=0, concat_axis=1, tiled=True),
    )
    seq_len = pair_all.shape[1]
    key_blocks = pair_all[0, :, :head_dim].reshape(seq_len // BLK, BLK, head_dim)
    value_blocks = pair_all[0, :, head_dim:].reshape(seq_len // BLK, BLK, head_dim)
    own_head = exp_index * head_group + ctx_index // query_parts
    own_part = ctx_index % query_parts
    per_shard = shard_len // BLK
    per_piece = piece_len // BLK
    local_count = ctx_count * per_piece
    source = jnp.arange(local_count, dtype=jnp.int32) // per_piece
    offset = jnp.arange(local_count, dtype=jnp.int32) % per_piece
    block_ids = source * per_shard + own_part * per_piece + offset
    head_pattern = lax.dynamic_index_in_dim(block_pattern, own_head, 0, keepdims=False)
    pattern_rows = jnp.take(head_pattern, block_ids, axis=0)
    q_blocks = query_all.reshape(local_count, BLK, head_dim)
    attended = attend_blocks(q_blocks, key_blocks, value_blocks, pattern_rows, block_ids)
    back_send = attended.reshape(ctx_count, piece_len, head_dim)
    heads_out = lax.all_to_all(back_send, "ctx", split_axis=0, concat_axis=0, tiled=True)
    head_rows = heads_out.reshape(head_group, shard_len, head_dim)
    out_weight = out_proj.reshape(head_group, head_dim, feat_width)
    tok_rows = shard_len // exp_count
    attn_sum = lax.psum_scatter(
        jnp.einsum("htd,hdm->tm", head_rows, out_weight, preferred_element_type=jnp.float32),
        "exp",
        scatter_dimension=0,
        tiled=True,
    )
    own_rows = lax.dynamic_slice_in_dim(inputs, exp_index * tok_rows, tok_rows, 0)
    residual = (own_rows.astype(jnp.float32) + attn_sum).astype(jnp.bfloat16)
    devices = ctx_count * exp_count
    experts = devices // 2
    capacity = 8 * tok_rows // experts
    moe_in = rms_scale(residual.astype(jnp.float32), moe_gain).astype(jnp.bfloat16)
    logits = jnp.dot(moe_in, router, preferred_element_type=jnp.float32)
    choose = expert_ids[:, :, None] == jnp.arange(experts, dtype=jnp.int32)[None, None, :]
    picked = jnp.sum(jnp.where(choose, logits[:, None, :], jnp.float32(0.0)), axis=2)
    gate_vals = jax.nn.sigmoid(picked)
    flat_hits = choose.reshape(-1, experts).astype(jnp.int32)
    running = jnp.cumsum(flat_hits, axis=0)
    slot_index = jnp.sum(running * flat_hits, axis=1) - 1
    target = expert_ids.reshape(-1) * capacity + slot_index
    placed = (jnp.arange(experts * capacity, dtype=jnp.int32)[:, None] == target[None, :]).reshape(
        experts * capacity, tok_rows, -1
    )
    dispatch = jnp.any(placed, axis=2).astype(jnp.bfloat16)
    send_rows = jnp.dot(dispatch, moe_in, preferred_element_type=jnp.float32).astype(jnp.bfloat16)
    send_rows = send_rows.reshape(experts, capacity, feat_width)
    own_pair = jnp.stack([gate_proj, up_proj], axis=0)
    other_pair = partner(own_pair, "exp", 0)
    other_down = partner(down_proj, "exp", 0)
    lower = exp_index % 2 == 0
    full_pair = jnp.where(
        lower,
        jnp.concatenate([own_pair, other_pair], axis=2),
        jnp.concatenate([other_pair, own_pair], axis=2),
    )
    full_down = jnp.where(
        lower,
        jnp.concatenate([down_proj, other_down], axis=0),
        jnp.concatenate([other_down, down_proj], axis=0),
    )
    halves = send_rows.reshape(devices, capacity // 2, feat_width)
    received = lax.all_to_all(halves, ("ctx", "exp"), split_axis=0, concat_axis=0, tiled=True)
    item_count = received.shape[1]
    row_vals = received.reshape(-1, feat_width)
    gate_act = jnp.dot(row_vals, full_pair[0], preferred_element_type=jnp.float32)
    up_act = jnp.dot(row_vals, full_pair[1], preferred_element_type=jnp.float32)
    hidden = (jax.nn.silu(gate_act) * up_act).astype(jnp.bfloat16)
    outputs = jnp.dot(hidden, full_down, preferred_element_type=jnp.float32)
    finished = outputs.astype(jnp.bfloat16).reshape(devices, item_count, feat_width)
    returned = lax.all_to_all(finished, ("ctx", "exp"), split_axis=0, concat_axis=0, tiled=True)
    expert_out = returned.reshape(experts, capacity, feat_width)
    gathered = jnp.take(expert_out.reshape(experts * capacity, feat_width), target, axis=0)
    gathered = gathered.reshape(tok_rows, -1, feat_width)
    moe_out = jnp.sum(gate_vals[:, :, None] * gathered.astype(jnp.float32), axis=1)
    return (residual.astype(jnp.float32) + moe_out).astype(jnp.bfloat16)


def solution(mesh):
    return jax.shard_map(
        body,
        mesh=mesh,
        in_specs=(
            P(None, "ctx", None),
            P(),
            P(),
            P(None, None, "exp", None),
            P("exp", None),
            P("exp", None),
            P("exp", None),
            P(),
            P(),
            P(None, ("ctx", "exp")),
            P(None, ("ctx", "exp")),
            P(("ctx", "exp"), None),
            P(("ctx", "exp"), None),
            P(),
        ),
        out_specs=P(("ctx", "exp"), None),
        check_vma=False,
    )
```

profile of v0, /device:TPU:0, one launch (start us, length us, event | category | flops | bytes accessed | tf_op | source)
XLA Modules:
  0.0 447.2 jit_solution(6870942828804241512)
XLA Ops:
  6.5 1.5 fusion.82
  8.1 7.6 %fusion.15 = (f32[512]{0:T(512)S(1)}, bf16[1,512,2048]{2,1,0:T(8,128)(2,1)S(1)}) fusion(bf16[4,512,2048]{2,1,0:T(8,128)(2,1)} %param.16, f32[]{:T(128)} %bitcast.3, f32[]{:T(128)} %bitcast.2, f32[]{:T(128)} %bitcast.1, f32[]{:T(128)} %bitcast), kind=kLoop, calls=%fused_computation.30 | loop fusion | flops 15728128 | bytes 10487824 | tf_op jit(solution)/shard_map/reduce_sum | solution.py:19
  15.7 0.0 copy-start.7
  15.8 3.5 fusion.38
  19.2 0.3 multiply_reduce_fusion.1
  19.6 0.1 fusion.57
  19.7 0.3 multiply_convert_fusion.2
  20.1 0.1 pad_maximum_fusion.1
  20.2 0.0 copy-start.8
  20.2 1.5 broadcast_in_dim.68
  21.7 7.3 %all-to-all-start.1 = ((bf16[8,512,256]{2,1,0:T(8,128)(2,1)}), bf16[8,512,256]{2,1,0:T(8,128)(2,1)}, u32[]{:S(2)}, u32[]{:S(2)}) async-start(bf16[8,512,256]{2,1,0:T(8,128)(2,1)} %bitcast.107), calls=%async_computation.1 | async-start | bytes 4194304 | tf_op jit(solution)/shard_map/all_to_all | solution.py:87
  28.9 0.7 constant_dynamic-slice_fusion
  29.6 0.1 copy.40
  29.8 0.6 gather_fusion
  30.4 0.1 select_compare_fusion
  30.4 0.1 reshape.366
  30.5 1.6 multiply_reduce_fusion.2
  32.2 1.1 multiply_convert_fusion.3
  33.3 44.0 %all-to-all-done.1 = bf16[8,512,256]{2,1,0:T(8,128)(2,1)} async-done(((bf16[8,512,256]{2,1,0:T(8,128)(2,1)}), bf16[8,512,256]{2,1,0:T(8,128)(2,1)}, u32[]{:S(2)}, u32[]{:S(2)}) %all-to-all-start.1) | async-done | bytes 2097184 | tf_op jit(solution)/shard_map/all_to_all | solution.py:87
  77.3 4.2 all-to-all-start
  81.5 0.0 reduce-scatter.2.cloned.1.call-start
  81.5 2.7 fusion.81
  84.2 4.2 gather_fusion.2
  88.4 3.1 gather_fusion.3
  91.5 4.2 all-to-all-done
  95.7 5.8 %fusion.13 = (f32[32,64]{1,0:T(8,128)S(1)}, f32[32,64,8,64]{1,3,2,0:T(8,128)S(1)}) fusion(pred[32,8]{1,0:T(8,128)(4,1)S(1)} %get-tuple-element.19, pred[32,8]{1,0:T(8,128)(4,1)S(1)} %get-tuple-element.18, bf16[32,64,128,1]{2,1,3,0:T(8,128)(2,1)} %bitcast.16, bf16[32,8,64,128]{3,2,1,0:T(8,128)(2,1)} %bitcast.110, pred[32,8]{1,0:T(8,128)(4,1)S(1)} %get-tuple-element.20), kind=kOutput, calls=%fused_computation.26 | convolution fusion | flops 276822016 | bytes 8921856 | tf_op jit(solution)/shard_map/nid,nkjd->nikj/dot_general | solution.py:30
  101.5 4.8 %divide_convert_fusion = bf16[32,64,128]{2,1,0:T(8,128)(2,1)S(1)} fusion(bf16[32,8,64,128]{3,2,1,0:T(8,128)(2,1)S(1)} %bitcast.109, pred[32,8]{1,0:T(8,128)(4,1)S(1)} %get-tuple-element.20, f32[32,64,8,64]{1,3,2,0:T(8,128)S(1)} %get-tuple-element.27, pred[32,8]{1,0:T(8,128)(4,1)S(1)} %get-tuple-element.19, pred[32,8]{1,0:T(8,128)(4,1)S(1)} %get-tuple-element.18, ...), kind=kOutput, calls=%fused_computation.69 | convolution fusion | flops 277348352 | bytes 8921856 | tf_op jit(solution)/shard_map/nikj,nkjd->nid/dot_general | solution.py:39
  106.4 18.0 %all_to_all.36 = bf16[8,256,128]{2,1,0:T(8,128)(2,1)S(1)} all-to-all(bf16[8,256,128]{2,1,0:T(8,128)(2,1)S(1)} %bitcast.114), channel_id=1, replica_groups=mesh['ctx'=8,'exp'=4] {'ctx'}, dimensions={0} | all-to-all | bytes 1048576 | tf_op jit(solution)/shard_map/all_to_all | solution.py:105
  124.3 3.3 convolution_bitcast_fusion
  127.7 0.0 reduce-scatter.2.cloned.1.call-update
  127.7 0.0 copy-start.5
  127.7 0.0 copy-start.6
  127.7 5.9 %pad_maximum_fusion = bf16[2,2048,704]{1,2,0:T(8,128)(2,1)} fusion(bf16[1,2048,704]{1,2,0:T(8,128)(2,1)} %bitcast.103, bf16[1,2048,704]{1,2,0:T(8,128)(2,1)} %bitcast.105), kind=kLoop, calls=%fused_computation.16 | loop fusion | flops 2883584 | bytes 11534336 | tf_op jit(solution)/shard_map/stack | solution.py:135
  133.6 0.0 collective-permute-start
  133.6 0.1 copy.44
  133.7 0.1 eq.72
  133.8 0.1 reshape.321
  134.0 1.7 reduce-window.6
  135.7 0.3 slice_reduce_fusion
  136.0 0.1 fusion.62
  136.1 0.1 sub.24
  136.2 0.1 copy.47
  136.3 0.5 fusion.29
  136.8 41.7 %reduce-scatter.2.cloned.1.call-done = f32[128,2048]{1,0:T(8,128)} async-done(((f32[512,2048]{1,0:T(8,128)}), f32[128,2048]{1,0:T(8,128)}) %reduce-scatter.2.cloned.1.call-update) | async-done | bytes 1048592 | tf_op jit(solution)/shard_map/reduce_scatter | solution.py:109
  178.5 1.6 fusion.48
  180.1 3.3 convolution_convert_fusion
  183.5 4.7 %all-to-all-start.3 = ((bf16[32,32,2048]{2,1,0:T(8,128)(2,1)}), bf16[32,32,2048]{2,1,0:T(8,128)(2,1)}, u32[]{:S(2)}, u32[]{:S(2)}) async-start(bf16[32,32,2048]{2,1,0:T(8,128)(2,1)} %bitcast.102), calls=%async_computation.4 | async-start | bytes 8388608 | tf_op jit(solution)/shard_map/all_to_all | solution.py:150
  188.2 0.2 collective-permute-start.1
  188.4 0.0 collective-permute-done
  188.4 14.2 %maximum_select_fusion = bf16[2,2048,1408]{1,2,0:T(8,128)(2,1)} fusion(bf16[2,2048,704]{1,2,0:T(8,128)(2,1)} %collective-permute-done, bf16[1,2048,704]{1,2,0:T(8,128)(2,1)} %bitcast.104, bf16[1,2048,704]{1,2,0:T(8,128)(2,1)} %bitcast.106, pred[]{:T(512)S(6)} %eq.79), kind=kLoop, calls=%fused_computation.4 | loop fusion | flops 74973184 | bytes 23068672 | tf_op jit(solution)/shard_map/jit(_where)/select_n | solution.py:139
  202.6 79.9 %all-to-all-done.3 = bf16[32,32,2048]{2,1,0:T(8,128)(2,1)} async-done(((bf16[32,32,2048]{2,1,0:T(8,128)(2,1)}), bf16[32,32,2048]{2,1,0:T(8,128)(2,1)}, u32[]{:S(2)}, u32[]{:S(2)}) %all-to-all-start.3) | async-done | bytes 4194336 | tf_op jit(solution)/shard_map/all_to_all | solution.py:150
  282.5 11.7 %fusion.4 = f32[1024,1408]{1,0:T(8,128)} fusion(bf16[1024,2048]{1,0:T(8,128)(2,1)} %bitcast.33, bf16[2,2048,1408]{1,2,0:T(8,128)(2,1)} %maximum_select_fusion), kind=kOutput, calls=%fused_computation.13 | convolution fusion | flops 5905580032 | bytes 15728640 | tf_op jit(solution)/shard_map/dot_general | solution.py:154
  294.3 23.0 %fusion.28 = bf16[1024,2048]{1,0:T(8,128)(2,1)} fusion(bf16[704,2048]{1,0:T(8,128)(2,1)} %collective-permute-done.1, bf16[704,2048]{1,0:T(8,128)(2,1)} %param.27, pred[]{:T(512)S(6)} %eq.79, f32[1024,1408]{1,0:T(8,128)} %fusion.4, bf16[1024,2048]{1,0:T(8,128)(2,1)} %bitcast.33, bf16[2,2048,1408]{1,2,0:T(8,128)(2,1)} %maximum_select_fusion), kind=kOutput, calls=%fused_computation.43 | convolution fusion | flops 11847860224 | bytes 25690112 | tf_op jit(solution)/shard_map/dot_general | solution.py:156
  317.3 5.6 %all-to-all-start.4 = ((bf16[32,32,2048]{2,1,0:T(8,128)(2,1)}), bf16[32,32,2048]{2,1,0:T(8,128)(2,1)}, u32[]{:S(2)}, u32[]{:S(2)}) async-start(bf16[32,32,2048]{2,1,0:T(8,128)(2,1)} %bitcast.108), calls=%async_computation.5 | async-start | bytes 8388608 | tf_op jit(solution)/shard_map/all_to_all | solution.py:158
  322.9 0.1 copy.49
  323.0 0.1 mul.237
  323.2 0.1 copy.48
  323.4 0.3 fusion.59
  323.7 0.1 copy.43
  323.9 93.3 %all-to-all-done.4 = bf16[32,32,2048]{2,1,0:T(8,128)(2,1)} async-done(((bf16[32,32,2048]{2,1,0:T(8,128)(2,1)}), bf16[32,32,2048]{2,1,0:T(8,128)(2,1)}, u32[]{:S(2)}, u32[]{:S(2)}) %all-to-all-start.4) | async-done | bytes 4194336 | tf_op jit(solution)/shard_map/all_to_all | solution.py:158
  417.1 9.9 %gather_fusion.1 = bf16[768,2048]{1,0:T(8,128)(2,1)} fusion(bf16[1024,2048]{1,0:T(8,128)(2,1)} %bitcast.39, s32[1024]{0:T(1024)S(1)} %pad_clamp_fusion), kind=kCustom, calls=%fused_computation.3 | custom fusion | bytes 6294528 | tf_op jit(solution)/shard_map/jit(_take)/gather | solution.py:160
  427.0 6.4 %gather.15 = bf16[128,6,2048]{2,1,0:T(8,128)(2,1)} reshape(bf16[768,2048]{1,0:T(8,128)(2,1)} %gather_fusion.1) | data formatting | bytes 6291456 | tf_op jit(solution)/shard_map/jit(_take)/gather | solution.py:160
  433.4 6.0 %multiply_reduce_fusion = f32[128,2048]{1,0:T(8,128)S(1)} fusion(bf16[128,6,2048]{2,1,0:T(8,128)(2,1)} %gather.15, f32[128,6]{1,0:T(8,128)S(1)} %copy.43, pred[128,6]{1,0:T(8,128)(4,1)S(1)} %copy.48), kind=kLoop, calls=%fused_computation.5 | loop fusion | flops 6029312 | bytes 4198144 | tf_op jit(solution)/shard_map/reduce_sum | solution.py:162
  439.4 0.9 fusion.51
  (41 shorter events, 0.3 us)
Async XLA Ops:
  6.5 117.8 %copy-start = (bf16[512,2048]{1,0:T(8,128)(2,1)S(1)}, bf16[512,2048]{1,0:T(8,128)(2,1)}, u32[]{:S(2)}) copy-start(bf16[512,2048]{1,0:T(8,128)(2,1)} %param.22) | copy-start | bytes 6291460
  8.1 7.7 %copy-start.9 = (bf16[2048,3,4,128]{3,2,1,0:T(4,128)(2,1)S(1)}, bf16[2048,3,4,128]{3,2,1,0:T(4,128)(2,1)}, u32[]{:S(2)}) copy-start(bf16[2048,3,4,128]{3,2,1,0:T(4,128)(2,1)} %param.19) | copy-start | bytes 18874372
  8.1 7.7 %copy-start.11 = (f32[2048]{0:T(1024)S(1)}, f32[2048]{0:T(1024)}, u32[]{:S(2)}) copy-start(f32[2048]{0:T(1024)} %param.18) | copy-start | bytes 24580
  15.7 3.5 copy-start.4
  15.7 4.0 copy-start.7
  19.2 2.5 copy-start.2
  20.2 12.0 %copy-start.8 = (f32[4,128]{1,0:T(4,128)S(1)}, f32[4,128]{1,0:T(4,128)}, u32[]{:S(2)}) copy-start(f32[4,128]{1,0:T(4,128)} %param.20) | copy-start | bytes 6148
  21.7 55.6 %all-to-all-start.1 = ((bf16[8,512,256]{2,1,0:T(8,128)(2,1)}), bf16[8,512,256]{2,1,0:T(8,128)(2,1)}, u32[]{:S(2)}, u32[]{:S(2)}) async-start(bf16[8,512,256]{2,1,0:T(8,128)(2,1)} %bitcast.107), calls=%async_computation.1 | async-start | bytes 4194304 | tf_op jit(solution)/shard_map/all_to_all | solution.py:87
  77.3 18.5 %all-to-all-start = ((bf16[8,256,128]{2,1,0:T(8,128)(2,1)}), bf16[8,256,128]{2,1,0:T(8,128)(2,1)}, u32[]{:S(2)}, u32[]{:S(2)}) async-start(bf16[8,256,128]{2,1,0:T(8,128)(2,1)} %multiply_convert_fusion.3), calls=%async_computation | async-start | bytes 1048576 | tf_op jit(solution)/shard_map/all_to_all | solution.py:86
  81.5 97.0 %reduce-scatter.2.cloned.1.call-start = ((), (), s32[]{:S(2)}) async-start(), calls=%async_computation.6 | async-start | bytes 5242880 | tf_op jit(solution)/shard_map/reduce_scatter | solution.py:109
  95.7 5.8 %copy-start.3 = (bf16[256,64,128]{2,1,0:T(8,128)(2,1)S(1)}, bf16[256,64,128]{2,1,0:T(8,128)(2,1)}, u32[]{:S(2)}) copy-start(bf16[256,64,128]{2,1,0:T(8,128)(2,1)} %gather_fusion.3) | copy-start | bytes 12582916
  127.7 5.9 %copy-start.5 = (s32[128,6]{0,1:T(8,128)S(1)}, s32[128,6]{0,1:T(8,128)}, u32[]{:S(2)}) copy-start(s32[128,6]{0,1:T(8,128)} %param.28) | copy-start | bytes 9220
  127.7 52.4 %copy-start.6 = (f32[2048]{0:T(1024)S(1)}, f32[2048]{0:T(1024)}, u32[]{:S(2)}) copy-start(f32[2048]{0:T(1024)} %param.23) | copy-start | bytes 24580
  133.6 54.9 %collective-permute-start = (bf16[2,2048,704]{1,2,0:T(8,128)(2,1)}, bf16[2,2048,704]{1,2,0:T(8,128)(2,1)}, u32[]{:S(2)}, u32[]{:S(2)}) collective-permute-start(bf16[2,2048,704]{1,2,0:T(8,128)(2,1)} %pad_maximum_fusion), channel_id=1, source_target_pairs={{0,1},{1,0},{2,3},{3,2},{4,5},{5,4},{6,7},{7,6},{8,9},{9,8},{10,11... | collective-permute-start | bytes 17301512 | tf_op jit(solution)/shard_map/ppermute | solution.py:15
  183.5 99.1 %all-to-all-start.3 = ((bf16[32,32,2048]{2,1,0:T(8,128)(2,1)}), bf16[32,32,2048]{2,1,0:T(8,128)(2,1)}, u32[]{:S(2)}, u32[]{:S(2)}) async-start(bf16[32,32,2048]{2,1,0:T(8,128)(2,1)} %bitcast.102), calls=%async_computation.4 | async-start | bytes 8388608 | tf_op jit(solution)/shard_map/all_to_all | solution.py:150
  188.2 106.1 %collective-permute-start.1 = (bf16[704,2048]{1,0:T(8,128)(2,1)}, bf16[704,2048]{1,0:T(8,128)(2,1)}, u32[]{:S(2)}, u32[]{:S(2)}) collective-permute-start(bf16[704,2048]{1,0:T(8,128)(2,1)} %param.27), channel_id=1, source_target_pairs={{0,1},{1,0},{2,3},{3,2},{4,5},{5,4},{6,7},{7,6},{8,9},{9,8},{10,11... | collective-permute-start | bytes 8650760 | tf_op jit(solution)/shard_map/ppermute | solution.py:15
  317.3 6.1 %copy-start.10 = (bf16[2048,16]{0,1:T(8,128)(2,1)S(1)}, bf16[2048,16]{0,1:T(8,128)(2,1)}, u32[]{:S(2)}) copy-start(bf16[2048,16]{0,1:T(8,128)(2,1)} %param.24) | copy-start | bytes 196612
  317.3 99.9 %all-to-all-start.4 = ((bf16[32,32,2048]{2,1,0:T(8,128)(2,1)}), bf16[32,32,2048]{2,1,0:T(8,128)(2,1)}, u32[]{:S(2)}, u32[]{:S(2)}) async-start(bf16[32,32,2048]{2,1,0:T(8,128)(2,1)} %bitcast.108), calls=%async_computation.5 | async-start | bytes 8388608 | tf_op jit(solution)/shard_map/all_to_all | solution.py:158
  427.0 13.3 %copy-start.1 = (bf16[512,2048]{1,0:T(8,128)(2,1)S(1)}, bf16[512,2048]{1,0:T(8,128)(2,1)}, u32[]{:S(2)}) copy-start(bf16[512,2048]{1,0:T(8,128)(2,1)} %param.22) | copy-start | bytes 6291460
Sparse Core Ops, SparseCore 0:
  127.8 50.6 reduce-scatter.1
where the time goes:
time: 448 us; the launch traced here: 447 us
  waiting for transfers between devices  263 us (59%)
  matrix products  55.8 us (12%)
  other arithmetic  42.3 us (9%)
  local copies, waits for them, and re-layouts  32.2 us (7%)
  starting transfers between devices  22 us (5%)
  blocking collectives  18 us (4%)
  between operations  13.8 us (3%)
    all_to_all x1, waiting for transfers between devices, body(): lax.all_to_all(finished, ('ctx', 'exp'), split_axis=0, concat_axis=0, til...  93.3 us
    all_to_all x1, waiting for transfers between devices, body(): lax.all_to_all(halves, ('ctx', 'exp'), split_axis=0, concat_axis=0, tiled...  79.9 us
    all_to_all x1, waiting for transfers between devices, body(): lax.all_to_all(pair_send, 'ctx', split_axis=0, concat_axis=1, tiled=True)  44 us
    reduce_scatter x1, waiting for transfers between devices, body(): lax.psum_scatter(jnp.einsum('htd,hdm->tm', head_rows, out_weight, preferr...  41.7 us
    dot_general x1, matrix products, body(): outputs = jnp.dot(hidden, full_down, preferred_element_type=jnp.float32)  23 us
    all_to_all x1, blocking collectives, body(): lax.all_to_all(back_send, 'ctx', split_axis=0, concat_axis=0, tiled=True)  18 us
    gather x2, local copies, waits for them, and re-layouts, body(): jnp.take(expert_out.reshape(experts * capacity, feat_width), target, axis=0)  16.3 us
    select_n x1, other arithmetic, body(): jnp.where(lower, jnp.concatenate([own_pair, other_pair], axis=2), jnp.con...  14.2 us
  transfers between devices with their start and end apart: 7, of which 5 were waited for; matrix products, arithmetic and copies ran while one was open for 12% of the time, Pallas kernels for 0%

commit v1 on v0

v1 whole, which is shorter than its diff:
```python
import jax
import jax.numpy as jnp
from jax import lax
from jax.experimental import pallas as pl
from jax.experimental.layout import Layout, with_layout_constraint
from jax.experimental.pallas import tpu as pltpu
from jax.sharding import Mesh
from jax.sharding import PartitionSpec as P

BLK = 64
EPSILON = 1e-06
F32 = jnp.float32
BF16 = jnp.bfloat16


def swap(value, axis, mask):
    if isinstance(axis, tuple):
        size = 1
        for name in axis:
            size *= lax.axis_size(name)
    else:
        size = lax.axis_size(axis)
    return lax.ppermute(value, axis, [(i, i ^ mask) for i in range(size)])


def shift(value, axis, by):
    size = lax.axis_size(axis)
    return lax.ppermute(value, axis, [(i, (i + by) % size) for i in range(size)])


def around(value, axis):
    size = lax.axis_size(axis)
    held = [value] + [None] * (size - 1)
    for step in range(1, size // 2 + 1):
        held[step] = shift(held[step - 1], axis, 1)
        if size - step > step:
            held[size - step] = shift(held[(size - step + 1) % size], axis, -1)
    return held


def pick(array, index):
    return lax.dynamic_index_in_dim(array, index, 0, keepdims=False)


def rms_scale(values, gain_vec):
    mean_sq = jnp.mean(values * values, axis=-1, keepdims=True)
    return values * lax.rsqrt(mean_sq + EPSILON) * gain_vec


def attend_kernel(at_ref, q_ref, kv_ref, seen_ref, out_ref):
    count, per_list = at_ref.shape
    head_dim = q_ref.shape[2]
    wide = per_list * BLK
    row_pos = lax.broadcasted_iota(jnp.int32, (BLK, wide), 0)
    col_pos = lax.broadcasted_iota(jnp.int32, (BLK, wide), 1)
    causal = (col_pos >= BLK) | (col_pos <= row_pos)

    def one(n):
        listed = jnp.concatenate([kv_ref[at_ref[n, j]] for j in range(per_list)], axis=0)
        scores = lax.dot_general(
            q_ref[n], listed[:, :head_dim], (((1,), (1,)), ((), ())), preferred_element_type=F32
        ) * (head_dim ** (-0.5))
        weights = jnp.where(causal & (seen_ref[n] > 0), jnp.exp(scores), F32(0.0))
        totals = jnp.sum(weights, axis=1, keepdims=True)
        summed = jnp.dot(weights.astype(BF16), listed[:, head_dim:], preferred_element_type=F32)
        out_ref[n] = (summed / totals).astype(BF16)

    together = 4 if count % 4 == 0 else 1

    def step(i, carry):
        for u in range(together):
            one(i * together + u)
        return carry

    lax.fori_loop(0, count // together, step, 0)


def attend(stored_at, q_blocks, kv_blocks, seen):
    whole = pl.BlockSpec(memory_space=pltpu.VMEM)
    n, width = stored_at.shape[0], stored_at.shape[1] * BLK
    head_dim = q_blocks.shape[2]
    return pl.pallas_call(
        attend_kernel,
        out_shape=jax.ShapeDtypeStruct(q_blocks.shape, BF16),
        in_specs=[pl.BlockSpec(memory_space=pltpu.SMEM), whole, whole, whole],
        out_specs=whole,
        compiler_params=pltpu.CompilerParams(vmem_limit_bytes=32 * 2**20),
        cost_estimate=pl.CostEstimate(
            flops=4 * n * BLK * width * head_dim,
            bytes_accessed=4 * kv_blocks.size,
            transcendentals=n * BLK * width,
        ),
    )(stored_at, q_blocks, kv_blocks, seen)


def expert_kernel(x_ref, g0, u0, d0, g1, u1, d1, out_ref, w_gate, w_up, w_down, hidden, partial, sems):
    copies = []
    for i, (src, dst) in enumerate(
        ((g0, w_gate.at[0]), (u0, w_up.at[0]), (d0, w_down.at[0]), (g1, w_gate.at[1]), (u1, w_up.at[1]), (d1, w_down.at[1]))
    ):
        copies.append(pltpu.make_async_copy(src, dst, sems.at[i]))
        copies[-1].start()
    across = (((1,), (1,)), ((), ()))
    count, feat = x_ref.shape
    tile = 256 if count % 256 == 0 else count
    wide = 512 if feat % 512 == 0 else feat
    for part in range(2):
        copies[3 * part].wait()
        copies[3 * part + 1].wait()

        @pl.loop(0, count // tile)
        def _(i):
            rows = pl.ds(pl.multiple_of(i * tile, tile), tile)
            gate_act = lax.dot_general(x_ref[rows, :], w_gate[part], across, preferred_element_type=F32)
            up_act = lax.dot_general(x_ref[rows, :], w_up[part], across, preferred_element_type=F32)
            hidden[rows, :] = (gate_act / (1.0 + jnp.exp(-gate_act)) * up_act).astype(BF16)

        copies[3 * part + 2].wait()

        @pl.loop(0, count // tile)
        def _(i):
            rows = pl.ds(pl.multiple_of(i * tile, tile), tile)
            for start in range(0, feat, wide):
                cols = slice(start, start + wide)
                term = jnp.dot(hidden[rows, :], w_down[part, :, cols], preferred_element_type=F32)
                if part == 0:
                    partial[rows, cols] = term
                else:
                    out_ref[rows, cols] = (partial[rows, cols] + term).astype(BF16)


def expert(rows, *weights):
    count, feat = rows.shape
    units = weights[0].shape[0]
    whole = pl.BlockSpec(memory_space=pltpu.VMEM)
    return pl.pallas_call(
        expert_kernel,
        out_shape=jax.ShapeDtypeStruct((count, feat), BF16),
        in_specs=[whole] + [pl.BlockSpec(memory_space=pl.ANY)] * 6,
        out_specs=whole,
        scratch_shapes=[
            pltpu.VMEM((2, units, feat), BF16),
            pltpu.VMEM((2, units, feat), BF16),
            pltpu.VMEM((2, units, feat), BF16),
            pltpu.VMEM((count, units), BF16),
            pltpu.VMEM((count, feat), F32),
            pltpu.SemaphoreType.DMA((6,)),
        ],
        compiler_params=pltpu.CompilerParams(vmem_limit_bytes=44 * 2**20),
        cost_estimate=pl.CostEstimate(
            flops=12 * count * feat * units,
            bytes_accessed=12 * feat * units + 4 * count * feat,
            transcendentals=2 * count * units,
        ),
    )(rows, *weights)


def body(
    stored,
    depth_weights,
    attn_gain,
    qkv_proj,
    q_gain,
    k_gain,
    out_proj,
    moe_gain,
    router,
    gate_proj,
    up_proj,
    down_proj,
    expert_ids,
    block_pattern,
):
    nz, nx, ne, ns = (lax.axis_size(name) for name in ("z", "x", "ep", "s"))
    iz, ix, ie, js = (lax.axis_index(name) for name in ("z", "x", "ep", "s"))
    depth_count, shard_len, feat = stored.shape
    head_dim = qkv_proj.shape[3]
    heads = qkv_proj.shape[2]
    tok = shard_len // (ne * ns)

    gate_proj, up_proj = gate_proj.T, up_proj.T
    gate_other = swap(gate_proj, "s", 1)
    up_other = swap(up_proj, "s", 1)
    down_other = swap(down_proj, "s", 1)
    ids = around(expert_ids, "z")

    blended = depth_weights[0] * stored[0].astype(F32)
    for depth_step in range(1, depth_count):
        blended = blended + depth_weights[depth_step] * stored[depth_step].astype(F32)
    inputs = blended.astype(BF16)
    normed = rms_scale(inputs.astype(F32), attn_gain).astype(BF16)
    projected = jnp.einsum("td,dche->chte", normed, qkv_proj, preferred_element_type=F32)
    projected = with_layout_constraint(projected, Layout(major_to_minor=(0, 1, 2, 3)))
    queries = rms_scale(projected[0], q_gain[:, None, :]).astype(BF16)
    keys = rms_scale(projected[1], k_gain[:, None, :]).astype(BF16)
    values = projected[2].astype(BF16)

    kv = jnp.concatenate([keys, values], axis=2)
    q_parts, kv_parts = [], []
    for m in range(nz):
        q_one, kv_one = pick(queries, iz ^ m), pick(kv, iz ^ m)
        if m:
            kv_one = swap(kv_one, "z", m)
            q_one = swap(q_one, "z", m)
        q_parts.append(q_one)
        pieces = [kv_one]
        step = 1
        while step < nx:
            pieces = pieces + [swap(piece, "x", step) for piece in pieces]
            step *= 2
        kv_parts.extend(pieces)
    kv_all = jnp.concatenate(kv_parts, axis=0)
    per_shard = shard_len // BLK
    kv_blocks = kv_all.reshape(-1, BLK, 2 * head_dim)
    own_head = (ie * ns + js) * heads + iz
    pattern = pick(block_pattern, own_head)
    pattern = pick(jnp.moveaxis(pattern.reshape(nz, nx, per_shard, -1), 1, 0), ix)
    pattern_rows = jnp.concatenate([pick(pattern, iz ^ m) for m in range(nz)], axis=0)
    safe_ids = jnp.maximum(pattern_rows, 0)
    shard = safe_ids // per_shard
    stored_at = (((shard // nx) ^ iz) * nx + ((shard % nx) ^ ix)) * per_shard + safe_ids % per_shard
    q_blocks = jnp.concatenate(q_parts, axis=0).reshape(-1, BLK, head_dim)
    seen = jnp.repeat((pattern_rows >= 0).astype(jnp.int32), BLK, axis=1)[:, None, :]
    attended = attend(stored_at, q_blocks, kv_blocks, seen).reshape(nz, shard_len, head_dim)

    out_weight = out_proj.reshape(heads, head_dim, feat)
    back = [attended[0]] + [swap(attended[m], "z", m) for m in range(1, nz)]
    weight_rows = jnp.concatenate([pick(out_weight, iz ^ m) for m in range(nz)], axis=0)
    attn_part = jnp.dot(jnp.concatenate(back, axis=1), weight_rows, preferred_element_type=F32)

    parts = attn_part.reshape(ne, ns, tok, feat)
    keep = lax.dynamic_index_in_dim(parts, js, 1, keepdims=False)
    give = lax.dynamic_index_in_dim(parts, js ^ 1, 1, keepdims=False).astype(BF16)
    pair_sum = keep + swap(give, "s", 1).astype(F32)
    attn_sum = pick(pair_sum, ie)
    for m in range(1, ne):
        attn_sum = attn_sum + swap(pick(pair_sum, ie ^ m).astype(BF16), "ep", m).astype(F32)

    own_rows = lax.dynamic_slice_in_dim(inputs, (ie * ns + js) * tok, tok, 0)
    residual = (own_rows.astype(F32) + attn_sum).astype(BF16)
    moe_in = rms_scale(residual.astype(F32), moe_gain).astype(BF16)

    plane = nx * ne
    me = ix * ne + ie
    experts = nz * plane
    capacity = 8 * tok // experts
    plane_ids = iz * plane + (jnp.arange(plane, dtype=jnp.int32) ^ me)
    before = (
        lax.broadcasted_iota(jnp.int32, (tok, tok), 0) > lax.broadcasted_iota(jnp.int32, (tok, tok), 1)
    ).astype(BF16)
    expert_cols = (jnp.arange(experts, dtype=jnp.int32)[:, None] == plane_ids[None, :]).astype(F32)

    def routing(ids_k):
        named = jnp.any(ids_k[:, :, None] == plane_ids[None, None, :], axis=1)
        order = jnp.dot(before, named.astype(BF16), preferred_element_type=F32)
        slots = jnp.where(named, order, F32(-1.0)).T
        steps = lax.broadcasted_iota(jnp.int32, (1, capacity, 1), 1).astype(F32)
        return (slots[:, None, :] == steps).reshape(plane * capacity, tok)

    places = [routing(ids_k) for ids_k in ids]
    chunks = around(moe_in, "z")

    def exchange(rows):
        rows = rows.reshape(plane, -1, feat)
        got = [rows[0]] + [swap(rows[m], ("x", "ep"), m) for m in range(1, plane)]
        return jnp.concatenate(got, axis=0)

    weights = (gate_proj, up_proj, down_proj, gate_other, up_other, down_other)

    def processed(group):
        sent = [
            jnp.dot(places[k].astype(BF16), chunks[k], preferred_element_type=F32)
            .astype(BF16)
            .reshape(plane, capacity, feat)
            for k in group
        ]
        done = exchange(expert(exchange(jnp.concatenate(sent, axis=1)), *weights))
        done = done.reshape(plane, len(group), capacity, feat)
        return {k: done[:, i].reshape(plane * capacity, feat) for i, k in enumerate(group)}

    def contribution(k, done):
        logits = jnp.dot(chunks[k], router, preferred_element_type=F32)
        gates = jax.nn.sigmoid(jnp.dot(logits, expert_cols, precision=lax.Precision.HIGHEST))
        gates = jnp.repeat(gates.T, capacity, axis=0)
        weight = jnp.where(places[k], gates, F32(0.0))
        high = weight.astype(BF16)
        low = (weight - high.astype(F32)).astype(BF16)
        over_rows = (((0,), (0,)), ((), ()))
        return lax.dot_general(high, done, over_rows, preferred_element_type=F32) + lax.dot_general(
            low, done, over_rows, preferred_element_type=F32
        )

    terms = [None] * nz
    half = nz // 2
    for group in (range(half), range(half, nz)):
        for k, done in processed(list(group)).items():
            terms[k] = contribution(k, done)

    total = terms[0]
    for indices, by in ((range(half, 0, -1), -1), (range(half + 1, nz), 1)):
        moving = None
        for k in indices:
            moving = terms[k] if moving is None else terms[k] + moving
            moving = shift(moving.astype(BF16), "z", by).astype(F32)
        if moving is not None:
            total = total + moving
    return (residual.astype(F32) + total).astype(BF16)


def solution(mesh):
    n_ctx, n_exp = mesh.shape["ctx"], mesh.shape["exp"]

    def fn(*args):
        far = args[3].shape[2] // n_exp
        split = Mesh(
            mesh.devices.reshape(far, n_ctx // far, n_exp // 2, 2), ("z", "x", "ep", "s")
        )
        ctx, exp, both = ("z", "x"), ("ep", "s"), ("z", "x", "ep", "s")
        return jax.shard_map(
            body,
            mesh=split,
            in_specs=(
                P(None, ctx, None),
                P(),
                P(),
                P(None, None, exp, None),
                P(exp, None),
                P(exp, None),
                P(exp, None),
                P(),
                P(),
                P(None, both),
                P(None, both),
                P(both, None),
                P(both, None),
                P(),
            ),
            out_specs=P(both, None),
            check_vma=False,
        )(*args)

    return fn
```

time: 448 us -> 264 us (0.59)
  waiting for transfers between devices: 263 us -> 130 us
  matrix products: 55.8 us -> 13.3 us
  starting transfers between devices: 22 us -> 57.1 us
  Pallas kernels: 0 us -> 34.1 us
  other arithmetic: 42.3 us -> 18.6 us
  local copies, waits for them, and re-layouts: 32.2 us -> 10 us
  blocking collectives: 18 us -> 0 us
  between operations: 13.8 us -> 0.59 us
    all_to_all x4 -> x0, waiting for transfers between devices: 221 us -> none  [the longest x1 93.3 us: body(): lax.all_to_all(finished, ('ctx', 'exp'), split_axis=0, concat_axis=0, til...]
    ppermute x2 -> x39, waiting for transfers between devices: 0.01 us -> 130 us  [the longest x30 67.7 us: swap(): return lax.ppermute(value, axis, [(i, i ^ mask) for i in range(size)])]
    ppermute x2 -> x39, starting transfers between devices: 0.25 us -> 57.1 us  [the longest x30 46.3 us: swap(): return lax.ppermute(value, axis, [(i, i ^ mask) for i in range(size)])]
    dot_general x8 -> x26, matrix products: 55.8 us -> 13.3 us  [the longest x1 3.46 us: body(): jnp.einsum('td,dche->chte', normed, qkv_proj, preferred_element_type=F32)]
    reduce_scatter x1 -> x0, waiting for transfers between devices: 41.7 us -> none  [body(): lax.psum_scatter(jnp.einsum('htd,hdm->tm', head_rows, out_weight, preferr...]
    pallas_call x0 -> x3, Pallas kernels: none -> 34.1 us  [the longest x2 26.7 us: expert(): pl.pallas_call(expert_kernel, out_shape=jax.ShapeDtypeStruct((count, feat...]
    gather x5 -> x0, local copies, waits for them, and re-layouts: 24.1 us -> none  [the longest x2 16.3 us: body(): jnp.take(expert_out.reshape(experts * capacity, feat_width), target, axis=0)]
    all_to_all x4 -> x0, starting transfers between devices: 21.7 us -> none  [the longest x1 7.25 us: body(): lax.all_to_all(pair_send, 'ctx', split_axis=0, concat_axis=1, tiled=True)]
  transfers between devices with their start and end apart: 7 -> 39, of which waited for: 5 -> 23; matrix products, arithmetic and copies ran while one was open for 12% -> 7% of each run, Pallas kernels for 0% -> 10%
where the time goes in v1:
time: 264 us
  waiting for transfers between devices  130 us (49%)
  starting transfers between devices  57.1 us (22%)
  Pallas kernels  34.1 us (13%)
  other arithmetic  18.6 us (7%)
  matrix products  13.3 us (5%)
  local copies, waits for them, and re-layouts  10 us (4%)
    ppermute x30, waiting for transfers between devices, swap(): return lax.ppermute(value, axis, [(i, i ^ mask) for i in range(size)])  67.7 us
    ppermute x9, waiting for transfers between devices, shift(): lax.ppermute(value, axis, [(i, (i + by) % size) for i in range(size)])  62.5 us
    ppermute x30, starting transfers between devices, swap(): return lax.ppermute(value, axis, [(i, i ^ mask) for i in range(size)])  46.3 us
    pallas_call x2, Pallas kernels, expert(): pl.pallas_call(expert_kernel, out_shape=jax.ShapeDtypeStruct((count, feat...  26.7 us
    ppermute x9, starting transfers between devices, shift(): lax.ppermute(value, axis, [(i, (i + by) % size) for i in range(size)])  10.8 us
    reduce_sum x3, other arithmetic, rms_scale(): mean_sq = jnp.mean(values * values, axis=-1, keepdims=True)  9.54 us
    pallas_call x1, Pallas kernels, attend(): pl.pallas_call(attend_kernel, out_shape=jax.ShapeDtypeStruct(q_blocks.sha...  7.42 us
  transfers between devices with their start and end apart: 39, of which 23 were waited for; matrix products, arithmetic and copies ran while one was open for 7% of the time, Pallas kernels for 10%

profile of v1, /device:TPU:0, one launch (start us, length us, event | category | flops | bytes accessed | tf_op | source)
XLA Modules:
  0.0 263.8 jit_solution(15945102594333093997)
XLA Ops:
  0.0 1.5 fusion.108
  1.5 7.6 %fusion.2 = (f32[512]{0:T(512)S(1)}, bf16[1,512,2048]{2,1,0:T(8,128)(2,1)S(1)}) fusion(bf16[4,512,2048]{2,1,0:T(8,128)(2,1)} %param.14, f32[]{:T(128)} %bitcast.3, f32[]{:T(128)} %bitcast.2, f32[]{:T(128)} %bitcast.1, f32[]{:T(128)} %bitcast), kind=kLoop, calls=%fused_computation.4 | loop fusion | flops 15728128 | bytes 10487824 | tf_op jit(solution)/shard_map/reduce_sum | solution.py:46
  9.1 3.5 %fusion.20 = f32[3,4,512,128]{3,2,1,0:T(8,128)S(1)} fusion(bf16[2048,3,4,128]{3,2,1,0:T(4,128)(2,1)S(1)} %copy-done.9, bf16[1,512,2048]{2,1,0:T(8,128)(2,1)S(1)} %get-tuple-element.16, f32[2048]{0:T(1024)S(1)} %copy-done.14, f32[512]{0:T(512)S(1)} %add_rsqrt_fusion.2), kind=kOutput, calls=%fused_computation.48 | convolution fusion | flops 3225419776 | bytes 11544576 | tf_op jit(solution)/shard_map/td,dche->chte/dot_general | solution.py:192
  13.3 0.7 multiply_convert_fusion
  14.0 0.8 dynamic-slice_bitcast_fusion.7
  14.8 5.0 %collective-permute-start.2 = (bf16[512,128]{1,0:T(8,128)(2,1)}, bf16[512,128]{1,0:T(8,128)(2,1)}, u32[]{:S(2)}, u32[]{:S(2)}) collective-permute-start(bf16[512,128]{1,0:T(8,128)(2,1)} %get-tuple-element.51), channel_id=1, source_target_pairs={{0,24},{8,16},{16,8},{24,0},{1,25},{9,17},{17,9},{25,1},{2,26},{10... | collective-permute-start | bytes 393224 | tf_op jit(solution)/shard_map/ppermute | solution.py:23
  20.5 0.7 constant_dynamic-update-slice_fusion.7
  21.2 1.7 collective-permute-start.3
  22.9 0.9 fusion.67
  23.8 1.2 collective-permute-start.4
  25.1 0.7 constant_dynamic-slice_fusion.4
  25.9 5.3 %collective-permute-start.6 = (bf16[512,256]{1,0:T(8,128)(2,1)}, bf16[512,256]{1,0:T(8,128)(2,1)S(1)}, u32[]{:S(2)}, u32[]{:S(2)}) collective-permute-start(bf16[512,256]{1,0:T(8,128)(2,1)} %get-tuple-element.45), channel_id=1, source_target_pairs={{0,16},{8,24},{16,0},{24,8},{1,17},{9,25},{17,1},{25,9},{2,18},{10... | collective-permute-start | bytes 786440 | tf_op jit(solution)/shard_map/ppermute | solution.py:23
  31.4 0.9 collective-permute-done.1
  32.3 2.7 %collective-permute-start.8 = (bf16[512,256]{1,0:T(8,128)(2,1)}, bf16[512,256]{1,0:T(8,128)(2,1)S(1)}, u32[]{:S(2)}, u32[]{:S(2)}) collective-permute-start(bf16[512,256]{1,0:T(8,128)(2,1)} %get-tuple-element.43), channel_id=1, source_target_pairs={{0,24},{8,16},{16,8},{24,0},{1,25},{9,17},{17,9},{25,1},{2,26},{10... | collective-permute-start | bytes 786440 | tf_op jit(solution)/shard_map/ppermute | solution.py:23
  35.0 3.6 %collective-permute-done.4 = bf16[512,256]{1,0:T(8,128)(2,1)S(1)} collective-permute-done((bf16[512,256]{1,0:T(8,128)(2,1)}, bf16[512,256]{1,0:T(8,128)(2,1)S(1)}, u32[]{:S(2)}, u32[]{:S(2)}) %collective-permute-start.4) | collective-permute-done | bytes 262176 | tf_op jit(solution)/shard_map/ppermute | solution.py:23
  38.6 1.5 collective-permute-start.5
  40.1 1.1 pad_maximum_fusion.6
  41.2 8.6 %collective-permute-done.6 = bf16[512,256]{1,0:T(8,128)(2,1)S(1)} collective-permute-done((bf16[512,256]{1,0:T(8,128)(2,1)}, bf16[512,256]{1,0:T(8,128)(2,1)S(1)}, u32[]{:S(2)}, u32[]{:S(2)}) %collective-permute-start.6) | collective-permute-done | bytes 262176 | tf_op jit(solution)/shard_map/ppermute | solution.py:23
  49.8 1.5 collective-permute-start.7
  52.1 5.3 %collective-permute-done.7 = bf16[512,256]{1,0:T(8,128)(2,1)S(1)} collective-permute-done((bf16[512,256]{1,0:T(8,128)(2,1)S(1)}, bf16[512,256]{1,0:T(8,128)(2,1)S(1)}, u32[]{:S(2)}, u32[]{:S(2)}) %collective-permute-start.7) | collective-permute-done | bytes 262176 | tf_op jit(solution)/shard_map/ppermute | solution.py:23
  57.4 2.8 %collective-permute-done.9 = bf16[512,256]{1,0:T(8,128)(2,1)S(1)} collective-permute-done((bf16[512,256]{1,0:T(8,128)(2,1)S(1)}, bf16[512,256]{1,0:T(8,128)(2,1)S(1)}, u32[]{:S(2)}, u32[]{:S(2)}) %collective-permute-start.9) | collective-permute-done | bytes 262176 | tf_op jit(solution)/shard_map/ppermute | solution.py:23
  60.2 7.4 %shard_map.136 = bf16[32,64,128]{2,1,0:T(8,128)(2,1)S(1)} custom-call(s32[32,8]{1,0:T(8,128)S(1)} %fusion.85.at_ref, bf16[32,64,128]{2,1,0:T(8,128)(2,1)S(1)} %bitcast.190, bf16[64,64,256]{2,1,0:T(8,128)(2,1)S(1)} %bitcast.189, s32[32,1,512]{2,1,0:T(1,128)S(1)} %broadcast_in_dim_reshape.3.seen_ref), custom_call_target="tpu_custom_call" | custom-call | flops 536870912 | bytes 4194304 | tf_op jit(solution)/shard_map/pallas_call | solution.py:82
  67.6 0.7 fusion.107
  68.3 1.9 collective-permute-start.12
  70.6 2.1 collective-permute-start.10
  72.7 1.2 dynamic-slice_bitcast_fusion.3
  73.9 2.3 collective-permute-done.12
  76.2 3.3 %collective-permute-done.11 = bf16[512,128]{1,0:T(8,128)(2,1)S(1)} collective-permute-done((bf16[512,128]{1,0:T(8,128)(2,1)S(1)}, bf16[512,128]{1,0:T(8,128)(2,1)S(1)}, u32[]{:S(2)}, u32[]{:S(2)}) %collective-permute-start.11) | collective-permute-done | bytes 131104 | tf_op jit(solution)/shard_map/ppermute | solution.py:23
  80.2 3.0 %fusion.9 = f32[512,2048]{1,0:T(8,128)S(1)} fusion(bf16[128,2048]{1,0:T(8,128)(2,1)} %get-tuple-element.40, bf16[128,2048]{1,0:T(8,128)(2,1)} %get-tuple-element.41, bf16[128,2048]{1,0:T(8,128)(2,1)} %get-tuple-element.42, bf16[128,2048]{1,0:T(8,128)(2,1)S(1)} %get-tuple-element.39, bf16[512,128]{1,0:T(8,128)(2,1)} %copy-done.11, ...), kind=kOutput, calls=%fused_computation.31 | convolution fusion | flops 1084227584 | bytes 6815744 | tf_op jit(solution)/shard_map/dot_general | solution.py:229
  83.2 1.3 fusion.41
  84.5 3.8 %collective-permute-start.28 = (s32[128,6]{0,1:T(8,128)S(1)}, s32[128,6]{0,1:T(8,128)S(1)}, u32[]{:S(2)}, u32[]{:S(2)}) collective-permute-start(s32[128,6]{0,1:T(8,128)S(1)} %copy-done.6), channel_id=1, source_target_pairs={{0,24},{8,0},{16,8},{24,16},{1,25},{9,1},{17,9},{25,17},{2,26},{10... | collective-permute-start | bytes 9224 | tf_op jit(solution)/shard_map/ppermute | solution.py:28
  88.9 1.1 collective-permute-done.15
  90.1 5.3 %collective-permute-done.26 = s32[128,6]{0,1:T(8,128)S(1)} collective-permute-done((s32[128,6]{0,1:T(8,128)S(1)}, s32[128,6]{0,1:T(8,128)S(1)}, u32[]{:S(2)}, u32[]{:S(2)}) %collective-permute-start.26) | collective-permute-done | bytes 3104 | tf_op jit(solution)/shard_map/ppermute | solution.py:28
  95.6 2.3 bitcast_add_fusion
  98.0 1.6 collective-permute-start.14
  100.2 9.9 %collective-permute-done.14 = bf16[128,2048]{1,0:T(8,128)(2,1)S(1)} collective-permute-done((bf16[128,2048]{1,0:T(8,128)(2,1)S(1)}, bf16[128,2048]{1,0:T(8,128)(2,1)S(1)}, u32[]{:S(2)}, u32[]{:S(2)}) %collective-permute-start.14) | collective-permute-done | bytes 524320 | tf_op jit(solution)/shard_map/ppermute | solution.py:23
  110.1 1.3 fusion.37
  111.7 3.8 %collective-permute-start.29 = (bf16[128,2048]{1,0:T(8,128)(2,1)S(1)}, bf16[128,2048]{1,0:T(8,128)(2,1)S(1)}, u32[]{:S(2)}, u32[]{:S(2)}) collective-permute-start(bf16[128,2048]{1,0:T(8,128)(2,1)S(1)} %fusion.39), channel_id=1, source_target_pairs={{0,24},{8,0},{16,8},{24,16},{1,25},{9,1},{17,9},{25,17},{2,26},{10... | collective-permute-start | bytes 1572872 | tf_op jit(solution)/shard_map/ppermute | solution.py:28
  116.4 11.9 %collective-permute-done.16 = bf16[128,2048]{1,0:T(8,128)(2,1)S(1)} collective-permute-done((bf16[128,2048]{1,0:T(8,128)(2,1)S(1)}, bf16[128,2048]{1,0:T(8,128)(2,1)S(1)}, u32[]{:S(2)}, u32[]{:S(2)}) %collective-permute-start.16) | collective-permute-done | bytes 524320 | tf_op jit(solution)/shard_map/ppermute | solution.py:28
  129.0 2.5 collective-permute-start.19
  131.8 2.3 collective-permute-done.29
  134.1 1.0 collective-permute-start.27
  136.2 11.7 %collective-permute-done.27 = bf16[128,2048]{1,0:T(8,128)(2,1)S(1)} collective-permute-done((bf16[128,2048]{1,0:T(8,128)(2,1)S(1)}, bf16[128,2048]{1,0:T(8,128)(2,1)S(1)}, u32[]{:S(2)}, u32[]{:S(2)}) %collective-permute-start.27) | collective-permute-done | bytes 524320 | tf_op jit(solution)/shard_map/ppermute | solution.py:28
  147.9 1.5 collective-permute-start.18
  149.3 1.5 collective-permute-start.17
  151.6 7.4 %collective-permute-done.18 = bf16[128,2048]{1,0:T(8,128)(2,1)S(1)} collective-permute-done((bf16[128,2048]{1,0:T(8,128)(2,1)S(1)}, bf16[128,2048]{1,0:T(8,128)(2,1)S(1)}, u32[]{:S(2)}, u32[]{:S(2)}) %collective-permute-start.18) | collective-permute-done | bytes 524320 | tf_op jit(solution)/shard_map/ppermute | solution.py:23
  159.0 3.5 %collective-permute-start.32 = (bf16[128,2048]{1,0:T(8,128)(2,1)S(1)}, bf16[128,2048]{1,0:T(8,128)(2,1)S(1)}, u32[]{:S(2)}, u32[]{:S(2)}) collective-permute-start(bf16[128,2048]{1,0:T(8,128)(2,1)S(1)} %get-tuple-element.37), channel_id=1, source_target_pairs={{0,6},{2,4},{4,2},{6,0},{1,7},{3,5},{5,3},{7,1},{8,14},{10,12},{12... | collective-permute-start | bytes 1572872 | tf_op jit(solution)/shard_map/ppermute | solution.py:23
  162.5 5.7 %collective-permute-done.17 = bf16[128,2048]{1,0:T(8,128)(2,1)S(1)} collective-permute-done((bf16[128,2048]{1,0:T(8,128)(2,1)S(1)}, bf16[128,2048]{1,0:T(8,128)(2,1)S(1)}, u32[]{:S(2)}, u32[]{:S(2)}) %collective-permute-start.17) | collective-permute-done | bytes 524320 | tf_op jit(solution)/shard_map/ppermute | solution.py:23
  168.4 2.6 collective-permute-start.30
  171.0 1.5 copy-done.10
  172.5 13.3 %shard_map.137 = bf16[512,2048]{1,0:T(8,128)(2,1)S(1)} custom-call(bf16[512,2048]{1,0:T(8,128)(2,1)S(1)} %pad_maximum_fusion.x_ref, bf16[704,2048]{1,0:T(8,128)(2,1)S(1)} %bitcast.192, bf16[704,2048]{1,0:T(8,128)(2,1)} %bitcast.54.u0, bf16[704,2048]{1,0:T(8,128)(2,1)} %d0.3, bf16[704,2048]{1,0:T(8,128)(2,1)} %collective-permute-done.20.g1, ...), custom_call_target="tpu_custom_call" | custom-call | flops 8858370048 | bytes 21495808 | tf_op jit(solution)/shard_map/pallas_call | solution.py:136
  186.6 1.5 collective-permute-start.25
  189.0 1.5 collective-permute-start.23
  191.3 13.3 %shard_map.138 = bf16[512,2048]{1,0:T(8,128)(2,1)S(1)} custom-call(bf16[512,2048]{1,0:T(8,128)(2,1)S(1)} %pad_maximum_fusion.2.x_ref, bf16[704,2048]{1,0:T(8,128)(2,1)S(1)} %bitcast.193, bf16[704,2048]{1,0:T(8,128)(2,1)} %bitcast.54.u0, bf16[704,2048]{1,0:T(8,128)(2,1)} %d0.3, bf16[704,2048]{1,0:T(8,128)(2,1)} %collective-permute-done.20.g1, ...), custom_call_target="tpu_custom_call" | custom-call | flops 8858370048 | bytes 21495808 | tf_op jit(solution)/shard_map/pallas_call | solution.py:136
  204.9 3.6 %collective-permute-start.35 = (bf16[128,2048]{1,0:T(8,128)(2,1)S(1)}, bf16[128,2048]{1,0:T(8,128)(2,1)S(1)}, u32[]{:S(2)}, u32[]{:S(2)}) collective-permute-start(bf16[128,2048]{1,0:T(8,128)(2,1)S(1)} %get-tuple-element.32), channel_id=1, source_target_pairs={{0,6},{2,4},{4,2},{6,0},{1,7},{3,5},{5,3},{7,1},{8,14},{10,12},{12... | collective-permute-start | bytes 1572872 | tf_op jit(solution)/shard_map/ppermute | solution.py:23
  208.5 0.9 collective-permute-start.34
  209.8 8.2 %collective-permute-done.23 = bf16[128,2048]{1,0:T(8,128)(2,1)S(1)} collective-permute-done((bf16[128,2048]{1,0:T(8,128)(2,1)S(1)}, bf16[128,2048]{1,0:T(8,128)(2,1)S(1)}, u32[]{:S(2)}, u32[]{:S(2)}) %collective-permute-start.23) | collective-permute-done | bytes 524320 | tf_op jit(solution)/shard_map/ppermute | solution.py:23
  218.9 3.0 %collective-permute-done.35 = bf16[128,2048]{1,0:T(8,128)(2,1)S(1)} collective-permute-done((bf16[128,2048]{1,0:T(8,128)(2,1)S(1)}, bf16[128,2048]{1,0:T(8,128)(2,1)S(1)}, u32[]{:S(2)}, u32[]{:S(2)}) %collective-permute-start.35) | collective-permute-done | bytes 524320 | tf_op jit(solution)/shard_map/ppermute | solution.py:23
  221.9 4.7 %collective-permute-done.34 = bf16[128,2048]{1,0:T(8,128)(2,1)S(1)} collective-permute-done((bf16[128,2048]{1,0:T(8,128)(2,1)S(1)}, bf16[128,2048]{1,0:T(8,128)(2,1)S(1)}, u32[]{:S(2)}, u32[]{:S(2)}) %collective-permute-start.34) | collective-permute-done | bytes 524320 | tf_op jit(solution)/shard_map/ppermute | solution.py:23
  226.5 1.0 collective-permute-done.33
  229.4 2.1 collective-permute-start.38
  231.4 21.7 %collective-permute-done.36 = bf16[128,2048]{1,0:T(8,128)(2,1)S(1)} collective-permute-done((bf16[128,2048]{1,0:T(8,128)(2,1)S(1)}, bf16[128,2048]{1,0:T(8,128)(2,1)S(1)}, u32[]{:S(2)}, u32[]{:S(2)}) %collective-permute-start.36) | collective-permute-done | bytes 524320 | tf_op jit(solution)/shard_map/ppermute | solution.py:28
  254.3 8.5 %collective-permute-done.37 = bf16[128,2048]{1,0:T(8,128)(2,1)S(1)} collective-permute-done((bf16[128,2048]{1,0:T(8,128)(2,1)S(1)}, bf16[128,2048]{1,0:T(8,128)(2,1)S(1)}, u32[]{:S(2)}, u32[]{:S(2)}) %collective-permute-start.37) | collective-permute-done | bytes 524320 | tf_op jit(solution)/shard_map/ppermute | solution.py:28
  262.7 1.1 fusion.40
  (125 shorter events, 15.9 us)
Async XLA Ops:
  0.0 115.5 %copy-start = (bf16[2048,16]{0,1:T(8,128)(2,1)S(1)}, bf16[2048,16]{0,1:T(8,128)(2,1)}, u32[]{:S(2)}) copy-start(bf16[2048,16]{0,1:T(8,128)(2,1)} %param.22) | copy-start | bytes 196612
  1.5 7.6 %copy-start.9 = (bf16[2048,3,4,128]{3,2,1,0:T(4,128)(2,1)S(1)}, bf16[2048,3,4,128]{3,2,1,0:T(4,128)(2,1)}, u32[]{:S(2)}) copy-start(bf16[2048,3,4,128]{3,2,1,0:T(4,128)(2,1)} %param.17) | copy-start | bytes 18874372
  1.5 7.6 %copy-start.14 = (f32[2048]{0:T(1024)S(1)}, f32[2048]{0:T(1024)}, u32[]{:S(2)}) copy-start(f32[2048]{0:T(1024)} %param.16) | copy-start | bytes 24580
  9.0 3.5 %copy-start.2 = (bf16[1,512,2048]{2,1,0:T(8,128)(2,1)}, bf16[1,512,2048]{2,1,0:T(8,128)(2,1)S(1)}, u32[]{:S(2)}) copy-start(bf16[1,512,2048]{2,1,0:T(8,128)(2,1)S(1)} %get-tuple-element.16) | copy-start | bytes 6291460
  12.6 0.7 copy-start.7
  12.6 0.7 copy-start.8
  14.8 11.1 %collective-permute-start.2 = (bf16[512,128]{1,0:T(8,128)(2,1)}, bf16[512,128]{1,0:T(8,128)(2,1)}, u32[]{:S(2)}, u32[]{:S(2)}) collective-permute-start(bf16[512,128]{1,0:T(8,128)(2,1)} %get-tuple-element.51), channel_id=1, source_target_pairs={{0,24},{8,16},{16,8},{24,0},{1,25},{9,17},{17,9},{25,1},{2,26},{10... | collective-permute-start | bytes 393224 | tf_op jit(solution)/shard_map/ppermute | solution.py:23
  19.8 12.4 %collective-permute-start.1 = (bf16[512,128]{1,0:T(8,128)(2,1)}, bf16[512,128]{1,0:T(8,128)(2,1)}, u32[]{:S(2)}, u32[]{:S(2)}) collective-permute-start(bf16[512,128]{1,0:T(8,128)(2,1)} %get-tuple-element.52), channel_id=1, source_target_pairs={{0,16},{8,24},{16,0},{24,8},{1,17},{9,25},{17,1},{25,9},{2,18},{10... | collective-permute-start | bytes 393224 | tf_op jit(solution)/shard_map/ppermute | solution.py:23
  19.8 20.3 %collective-permute-start = (bf16[512,128]{1,0:T(8,128)(2,1)S(1)}, bf16[512,128]{1,0:T(8,128)(2,1)}, u32[]{:S(2)}, u32[]{:S(2)}) collective-permute-start(bf16[512,128]{1,0:T(8,128)(2,1)S(1)} %get-tuple-element.53), channel_id=1, source_target_pairs={{0,8},{8,0},{16,24},{24,16},{1,9},{9,1},{17,25},{25,17},{2,10},{10... | collective-permute-start | bytes 393224 | tf_op jit(solution)/shard_map/ppermute | solution.py:23
  21.2 30.1 %collective-permute-start.3 = (bf16[512,256]{1,0:T(8,128)(2,1)}, bf16[512,256]{1,0:T(8,128)(2,1)S(1)}, u32[]{:S(2)}, u32[]{:S(2)}) collective-permute-start(bf16[512,256]{1,0:T(8,128)(2,1)} %get-tuple-element.14), channel_id=1, source_target_pairs={{0,4},{4,0},{1,5},{5,1},{2,6},{6,2},{3,7},{7,3},{8,12},{12,8},{9,1... | collective-permute-start | bytes 786440 | tf_op jit(solution)/shard_map/ppermute | solution.py:23
  23.8 14.8 %collective-permute-start.4 = (bf16[512,256]{1,0:T(8,128)(2,1)}, bf16[512,256]{1,0:T(8,128)(2,1)S(1)}, u32[]{:S(2)}, u32[]{:S(2)}) collective-permute-start(bf16[512,256]{1,0:T(8,128)(2,1)} %get-tuple-element.44), channel_id=1, source_target_pairs={{0,8},{8,0},{16,24},{24,16},{1,9},{9,1},{17,25},{25,17},{2,10},{10... | collective-permute-start | bytes 786440 | tf_op jit(solution)/shard_map/ppermute | solution.py:23
  25.9 23.9 %collective-permute-start.6 = (bf16[512,256]{1,0:T(8,128)(2,1)}, bf16[512,256]{1,0:T(8,128)(2,1)S(1)}, u32[]{:S(2)}, u32[]{:S(2)}) collective-permute-start(bf16[512,256]{1,0:T(8,128)(2,1)} %get-tuple-element.45), channel_id=1, source_target_pairs={{0,16},{8,24},{16,0},{24,8},{1,17},{9,25},{17,1},{25,9},{2,18},{10... | collective-permute-start | bytes 786440 | tf_op jit(solution)/shard_map/ppermute | solution.py:23
  32.3 19.1 %collective-permute-start.8 = (bf16[512,256]{1,0:T(8,128)(2,1)}, bf16[512,256]{1,0:T(8,128)(2,1)S(1)}, u32[]{:S(2)}, u32[]{:S(2)}) collective-permute-start(bf16[512,256]{1,0:T(8,128)(2,1)} %get-tuple-element.43), channel_id=1, source_target_pairs={{0,24},{8,16},{16,8},{24,0},{1,25},{9,17},{17,9},{25,1},{2,26},{10... | collective-permute-start | bytes 786440 | tf_op jit(solution)/shard_map/ppermute | solution.py:23
  38.6 13.4 %collective-permute-start.5 = (bf16[512,256]{1,0:T(8,128)(2,1)S(1)}, bf16[512,256]{1,0:T(8,128)(2,1)S(1)}, u32[]{:S(2)}, u32[]{:S(2)}) collective-permute-start(bf16[512,256]{1,0:T(8,128)(2,1)S(1)} %collective-permute-done.4), channel_id=1, source_target_pairs={{0,4},{4,0},{1,5},{5,1},{2,6},{6,2},{3,7},{7,3},{8,12},{12,8},{9,1... | collective-permute-start | bytes 786440 | tf_op jit(solution)/shard_map/ppermute | solution.py:23
  49.8 7.5 %collective-permute-start.7 = (bf16[512,256]{1,0:T(8,128)(2,1)S(1)}, bf16[512,256]{1,0:T(8,128)(2,1)S(1)}, u32[]{:S(2)}, u32[]{:S(2)}) collective-permute-start(bf16[512,256]{1,0:T(8,128)(2,1)S(1)} %collective-permute-done.6), channel_id=1, source_target_pairs={{0,4},{4,0},{1,5},{5,1},{2,6},{6,2},{3,7},{7,3},{8,12},{12,8},{9,1... | collective-permute-start | bytes 786440 | tf_op jit(solution)/shard_map/ppermute | solution.py:23
  51.4 8.7 %collective-permute-start.9 = (bf16[512,256]{1,0:T(8,128)(2,1)S(1)}, bf16[512,256]{1,0:T(8,128)(2,1)S(1)}, u32[]{:S(2)}, u32[]{:S(2)}) collective-permute-start(bf16[512,256]{1,0:T(8,128)(2,1)S(1)} %collective-permute-done.8), channel_id=1, source_target_pairs={{0,4},{4,0},{1,5},{5,1},{2,6},{6,2},{3,7},{7,3},{8,12},{12,8},{9,1... | collective-permute-start | bytes 786440 | tf_op jit(solution)/shard_map/ppermute | solution.py:23
  60.1 12.6 %copy-start.4 = (bf16[512,2048]{1,0:T(8,128)(2,1)S(1)}, bf16[512,2048]{1,0:T(8,128)(2,1)}, u32[]{:S(2)}) copy-start(bf16[512,2048]{1,0:T(8,128)(2,1)} %param.20) | copy-start | bytes 6291460
  68.3 7.9 %collective-permute-start.12 = (bf16[512,128]{1,0:T(8,128)(2,1)S(1)}, bf16[512,128]{1,0:T(8,128)(2,1)S(1)}, u32[]{:S(2)}, u32[]{:S(2)}) collective-permute-start(bf16[512,128]{1,0:T(8,128)(2,1)S(1)} %bitcast.222), channel_id=1, source_target_pairs={{0,24},{8,16},{16,8},{24,0},{1,25},{9,17},{17,9},{25,1},{2,26},{10... | collective-permute-start | bytes 393224 | tf_op jit(solution)/shard_map/ppermute | solution.py:23
  70.2 9.2 %collective-permute-start.11 = (bf16[512,128]{1,0:T(8,128)(2,1)S(1)}, bf16[512,128]{1,0:T(8,128)(2,1)S(1)}, u32[]{:S(2)}, u32[]{:S(2)}) collective-permute-start(bf16[512,128]{1,0:T(8,128)(2,1)S(1)} %bitcast.221), channel_id=1, source_target_pairs={{0,16},{8,24},{16,0},{24,8},{1,17},{9,25},{17,1},{25,9},{2,18},{10... | collective-permute-start | bytes 393224 | tf_op jit(solution)/shard_map/ppermute | solution.py:23
  70.6 8.8 %collective-permute-start.10 = (bf16[512,128]{1,0:T(8,128)(2,1)S(1)}, bf16[512,128]{1,0:T(8,128)(2,1)S(1)}, u32[]{:S(2)}, u32[]{:S(2)}) collective-permute-start(bf16[512,128]{1,0:T(8,128)(2,1)S(1)} %bitcast.220), channel_id=1, source_target_pairs={{0,8},{8,0},{16,24},{24,16},{1,9},{9,1},{17,25},{25,17},{2,10},{10... | collective-permute-start | bytes 393224 | tf_op jit(solution)/shard_map/ppermute | solution.py:23
  76.2 3.3 %copy-start.11 = (bf16[512,128]{1,0:T(8,128)(2,1)}, bf16[512,128]{1,0:T(8,128)(2,1)S(1)}, u32[]{:S(2)}) copy-start(bf16[512,128]{1,0:T(8,128)(2,1)S(1)} %collective-permute-done.12) | copy-start | bytes 393220
  79.5 0.7 copy-start.12
  79.5 0.7 copy-start.13
  80.2 8.2 %copy-start.1 = (bf16[2048,704]{0,1:T(8,128)(2,1)S(1)}, bf16[2048,704]{0,1:T(8,128)(2,1)}, u32[]{:S(2)}) copy-start(bf16[2048,704]{0,1:T(8,128)(2,1)} %param.23) | copy-start | bytes 8650756
  83.2 5.2 %copy-start.3 = (f32[512,2048]{1,0:T(8,128)}, f32[512,2048]{1,0:T(8,128)S(1)}, u32[]{:S(2)}) copy-start(f32[512,2048]{1,0:T(8,128)S(1)} %fusion.9) | copy-start | bytes 12582916
  83.2 1.3 copy-start.6
  84.5 11.1 %collective-permute-start.13 = (bf16[2,128,2048]{2,1,0:T(8,128)(2,1)}, bf16[2,128,2048]{2,1,0:T(8,128)(2,1)}, u32[]{:S(2)}, u32[]{:S(2)}) collective-permute-start(bf16[2,128,2048]{2,1,0:T(8,128)(2,1)} %fusion.41), channel_id=1, source_target_pairs={{0,1},{1,0},{2,3},{3,2},{4,5},{5,4},{6,7},{7,6},{8,9},{9,8},{10,11... | collective-permute-start | bytes 3145736 | tf_op jit(solution)/shard_map/ppermute | solution.py:23
  84.5 5.4 %collective-permute-start.15 = (s32[128,6]{0,1:T(8,128)S(1)}, s32[128,6]{0,1:T(8,128)S(1)}, u32[]{:S(2)}, u32[]{:S(2)}) collective-permute-start(s32[128,6]{0,1:T(8,128)S(1)} %copy-done.6), channel_id=1, source_target_pairs={{0,8},{8,16},{16,24},{24,0},{1,9},{9,17},{17,25},{25,1},{2,10},{10... | collective-permute-start | bytes 9224 | tf_op jit(solution)/shard_map/ppermute | solution.py:28
  84.5 5.5 %collective-permute-start.28 = (s32[128,6]{0,1:T(8,128)S(1)}, s32[128,6]{0,1:T(8,128)S(1)}, u32[]{:S(2)}, u32[]{:S(2)}) collective-permute-start(s32[128,6]{0,1:T(8,128)S(1)} %copy-done.6), channel_id=1, source_target_pairs={{0,24},{8,0},{16,8},{24,16},{1,25},{9,1},{17,9},{25,17},{2,26},{10... | collective-permute-start | bytes 9224 | tf_op jit(solution)/shard_map/ppermute | solution.py:28
  88.4 80.0 %collective-permute-start.20 = (bf16[704,2048]{1,0:T(8,128)(2,1)S(1)}, bf16[704,2048]{1,0:T(8,128)(2,1)}, u32[]{:S(2)}, u32[]{:S(2)}) collective-permute-start(bf16[704,2048]{1,0:T(8,128)(2,1)S(1)} %bitcast.191), channel_id=1, source_target_pairs={{0,1},{1,0},{2,3},{3,2},{4,5},{5,4},{6,7},{7,6},{8,9},{9,8},{10,11... | collective-permute-start | bytes 8650760 | tf_op jit(solution)/shard_map/ppermute | solution.py:23
  88.4 82.6 %collective-permute-start.21 = (bf16[704,2048]{1,0:T(8,128)(2,1)}, bf16[704,2048]{1,0:T(8,128)(2,1)}, u32[]{:S(2)}, u32[]{:S(2)}) collective-permute-start(bf16[704,2048]{1,0:T(8,128)(2,1)} %bitcast.54.u0), channel_id=1, source_target_pairs={{0,1},{1,0},{2,3},{3,2},{4,5},{5,4},{6,7},{7,6},{8,9},{9,8},{10,11... | collective-permute-start | bytes 8650760 | tf_op jit(solution)/shard_map/ppermute | solution.py:23
  90.0 5.4 %collective-permute-start.26 = (s32[128,6]{0,1:T(8,128)S(1)}, s32[128,6]{0,1:T(8,128)S(1)}, u32[]{:S(2)}, u32[]{:S(2)}) collective-permute-start(s32[128,6]{0,1:T(8,128)S(1)} %collective-permute-done.15), channel_id=1, source_target_pairs={{0,8},{8,16},{16,24},{24,0},{1,9},{9,17},{17,25},{25,1},{2,10},{10... | collective-permute-start | bytes 9224 | tf_op jit(solution)/shard_map/ppermute | solution.py:28
  90.1 80.9 %collective-permute-start.22 = (bf16[704,2048]{1,0:T(8,128)(2,1)}, bf16[704,2048]{1,0:T(8,128)(2,1)S(1)}, u32[]{:S(2)}, u32[]{:S(2)}) collective-permute-start(bf16[704,2048]{1,0:T(8,128)(2,1)} %d0.3), channel_id=1, source_target_pairs={{0,1},{1,0},{2,3},{3,2},{4,5},{5,4},{6,7},{7,6},{8,9},{9,8},{10,11... | collective-permute-start | bytes 8650760 | tf_op jit(solution)/shard_map/ppermute | solution.py:23
  97.9 13.5 %copy-start.5 = (f32[2048]{0:T(1024)S(1)}, f32[2048]{0:T(1024)}, u32[]{:S(2)}) copy-start(f32[2048]{0:T(1024)} %param.21) | copy-start | bytes 24580
  98.0 12.1 %collective-permute-start.14 = (bf16[128,2048]{1,0:T(8,128)(2,1)S(1)}, bf16[128,2048]{1,0:T(8,128)(2,1)S(1)}, u32[]{:S(2)}, u32[]{:S(2)}) collective-permute-start(bf16[128,2048]{1,0:T(8,128)(2,1)S(1)} %fusion.43), channel_id=1, source_target_pairs={{0,2},{2,0},{1,3},{3,1},{4,6},{6,4},{5,7},{7,5},{8,10},{10,8},{9,1... | collective-permute-start | bytes 1572872 | tf_op jit(solution)/shard_map/ppermute | solution.py:23
  111.6 16.7 %collective-permute-start.16 = (bf16[128,2048]{1,0:T(8,128)(2,1)S(1)}, bf16[128,2048]{1,0:T(8,128)(2,1)S(1)}, u32[]{:S(2)}, u32[]{:S(2)}) collective-permute-start(bf16[128,2048]{1,0:T(8,128)(2,1)S(1)} %fusion.39), channel_id=1, source_target_pairs={{0,8},{8,16},{16,24},{24,0},{1,9},{9,17},{17,25},{25,1},{2,10},{10... | collective-permute-start | bytes 1572872 | tf_op jit(solution)/shard_map/ppermute | solution.py:28
  111.7 22.4 %collective-permute-start.29 = (bf16[128,2048]{1,0:T(8,128)(2,1)S(1)}, bf16[128,2048]{1,0:T(8,128)(2,1)S(1)}, u32[]{:S(2)}, u32[]{:S(2)}) collective-permute-start(bf16[128,2048]{1,0:T(8,128)(2,1)S(1)} %fusion.39), channel_id=1, source_target_pairs={{0,24},{8,0},{16,8},{24,16},{1,25},{9,1},{17,9},{25,17},{2,26},{10... | collective-permute-start | bytes 1572872 | tf_op jit(solution)/shard_map/ppermute | solution.py:28
  129.0 20.3 %collective-permute-start.19 = (bf16[128,2048]{1,0:T(8,128)(2,1)S(1)}, bf16[128,2048]{1,0:T(8,128)(2,1)S(1)}, u32[]{:S(2)}, u32[]{:S(2)}) collective-permute-start(bf16[128,2048]{1,0:T(8,128)(2,1)S(1)} %get-tuple-element.29), channel_id=1, source_target_pairs={{0,6},{2,4},{4,2},{6,0},{1,7},{3,5},{5,3},{7,1},{8,14},{10,12},{12... | collective-permute-start | bytes 1572872 | tf_op jit(solution)/shard_map/ppermute | solution.py:23
  134.1 13.8 %collective-permute-start.27 = (bf16[128,2048]{1,0:T(8,128)(2,1)S(1)}, bf16[128,2048]{1,0:T(8,128)(2,1)S(1)}, u32[]{:S(2)}, u32[]{:S(2)}) collective-permute-start(bf16[128,2048]{1,0:T(8,128)(2,1)S(1)} %collective-permute-done.16), channel_id=1, source_target_pairs={{0,8},{8,16},{16,24},{24,0},{1,9},{9,17},{17,25},{25,1},{2,10},{10... | collective-permute-start | bytes 1572872 | tf_op jit(solution)/shard_map/ppermute | solution.py:28
  147.9 11.1 %collective-permute-start.18 = (bf16[128,2048]{1,0:T(8,128)(2,1)S(1)}, bf16[128,2048]{1,0:T(8,128)(2,1)S(1)}, u32[]{:S(2)}, u32[]{:S(2)}) collective-permute-start(bf16[128,2048]{1,0:T(8,128)(2,1)S(1)} %get-tuple-element.30), channel_id=1, source_target_pairs={{0,4},{2,6},{4,0},{6,2},{1,5},{3,7},{5,1},{7,3},{8,12},{10,14},{12... | collective-permute-start | bytes 1572872 | tf_op jit(solution)/shard_map/ppermute | solution.py:23
  149.3 18.8 %collective-permute-start.17 = (bf16[128,2048]{1,0:T(8,128)(2,1)S(1)}, bf16[128,2048]{1,0:T(8,128)(2,1)S(1)}, u32[]{:S(2)}, u32[]{:S(2)}) collective-permute-start(bf16[128,2048]{1,0:T(8,128)(2,1)S(1)} %get-tuple-element.28), channel_id=1, source_target_pairs={{0,2},{2,0},{4,6},{6,4},{1,3},{3,1},{5,7},{7,5},{8,10},{10,8},{12,... | collective-permute-start | bytes 1572872 | tf_op jit(solution)/shard_map/ppermute | solution.py:23
  159.0 30.0 %collective-permute-start.32 = (bf16[128,2048]{1,0:T(8,128)(2,1)S(1)}, bf16[128,2048]{1,0:T(8,128)(2,1)S(1)}, u32[]{:S(2)}, u32[]{:S(2)}) collective-permute-start(bf16[128,2048]{1,0:T(8,128)(2,1)S(1)} %get-tuple-element.37), channel_id=1, source_target_pairs={{0,6},{2,4},{4,2},{6,0},{1,7},{3,5},{5,3},{7,1},{8,14},{10,12},{12... | collective-permute-start | bytes 1572872 | tf_op jit(solution)/shard_map/ppermute | solution.py:23
  168.1 22.3 %collective-permute-start.31 = (bf16[128,2048]{1,0:T(8,128)(2,1)S(1)}, bf16[128,2048]{1,0:T(8,128)(2,1)S(1)}, u32[]{:S(2)}, u32[]{:S(2)}) collective-permute-start(bf16[128,2048]{1,0:T(8,128)(2,1)S(1)} %get-tuple-element.38), channel_id=1, source_target_pairs={{0,4},{2,6},{4,0},{6,2},{1,5},{3,7},{5,1},{7,3},{8,12},{10,14},{12... | collective-permute-start | bytes 1572872 | tf_op jit(solution)/shard_map/ppermute | solution.py:23
  168.4 22.7 %collective-permute-start.30 = (bf16[128,2048]{1,0:T(8,128)(2,1)S(1)}, bf16[128,2048]{1,0:T(8,128)(2,1)S(1)}, u32[]{:S(2)}, u32[]{:S(2)}) collective-permute-start(bf16[128,2048]{1,0:T(8,128)(2,1)S(1)} %get-tuple-element.36), channel_id=1, source_target_pairs={{0,2},{2,0},{4,6},{6,4},{1,3},{3,1},{5,7},{7,5},{8,10},{10,8},{12,... | collective-permute-start | bytes 1572872 | tf_op jit(solution)/shard_map/ppermute | solution.py:23
  171.0 1.5 copy-start.10
  186.6 22.8 %collective-permute-start.25 = (bf16[128,2048]{1,0:T(8,128)(2,1)S(1)}, bf16[128,2048]{1,0:T(8,128)(2,1)S(1)}, u32[]{:S(2)}, u32[]{:S(2)}) collective-permute-start(bf16[128,2048]{1,0:T(8,128)(2,1)S(1)} %get-tuple-element.24), channel_id=1, source_target_pairs={{0,6},{2,4},{4,2},{6,0},{1,7},{3,5},{5,3},{7,1},{8,14},{10,12},{12... | collective-permute-start | bytes 1572872 | tf_op jit(solution)/shard_map/ppermute | solution.py:23
  188.1 21.8 %collective-permute-start.24 = (bf16[128,2048]{1,0:T(8,128)(2,1)S(1)}, bf16[128,2048]{1,0:T(8,128)(2,1)S(1)}, u32[]{:S(2)}, u32[]{:S(2)}) collective-permute-start(bf16[128,2048]{1,0:T(8,128)(2,1)S(1)} %get-tuple-element.25), channel_id=1, source_target_pairs={{0,4},{2,6},{4,0},{6,2},{1,5},{3,7},{5,1},{7,3},{8,12},{10,14},{12... | collective-permute-start | bytes 1572872 | tf_op jit(solution)/shard_map/ppermute | solution.py:23
  189.0 29.1 %collective-permute-start.23 = (bf16[128,2048]{1,0:T(8,128)(2,1)S(1)}, bf16[128,2048]{1,0:T(8,128)(2,1)S(1)}, u32[]{:S(2)}, u32[]{:S(2)}) collective-permute-start(bf16[128,2048]{1,0:T(8,128)(2,1)S(1)} %get-tuple-element.26), channel_id=1, source_target_pairs={{0,2},{2,0},{4,6},{6,4},{1,3},{3,1},{5,7},{7,5},{8,10},{10,8},{12,... | collective-permute-start | bytes 1572872 | tf_op jit(solution)/shard_map/ppermute | solution.py:23
  204.9 17.0 %collective-permute-start.35 = (bf16[128,2048]{1,0:T(8,128)(2,1)S(1)}, bf16[128,2048]{1,0:T(8,128)(2,1)S(1)}, u32[]{:S(2)}, u32[]{:S(2)}) collective-permute-start(bf16[128,2048]{1,0:T(8,128)(2,1)S(1)} %get-tuple-element.32), channel_id=1, source_target_pairs={{0,6},{2,4},{4,2},{6,0},{1,7},{3,5},{5,3},{7,1},{8,14},{10,12},{12... | collective-permute-start | bytes 1572872 | tf_op jit(solution)/shard_map/ppermute | solution.py:23
  208.5 18.0 %collective-permute-start.34 = (bf16[128,2048]{1,0:T(8,128)(2,1)S(1)}, bf16[128,2048]{1,0:T(8,128)(2,1)S(1)}, u32[]{:S(2)}, u32[]{:S(2)}) collective-permute-start(bf16[128,2048]{1,0:T(8,128)(2,1)S(1)} %get-tuple-element.33), channel_id=1, source_target_pairs={{0,4},{2,6},{4,0},{6,2},{1,5},{3,7},{5,1},{7,3},{8,12},{10,14},{12... | collective-permute-start | bytes 1572872 | tf_op jit(solution)/shard_map/ppermute | solution.py:23
  209.4 18.2 %collective-permute-start.33 = (bf16[128,2048]{1,0:T(8,128)(2,1)S(1)}, bf16[128,2048]{1,0:T(8,128)(2,1)S(1)}, u32[]{:S(2)}, u32[]{:S(2)}) collective-permute-start(bf16[128,2048]{1,0:T(8,128)(2,1)S(1)} %get-tuple-element.34), channel_id=1, source_target_pairs={{0,2},{2,0},{4,6},{6,4},{1,3},{3,1},{5,7},{7,5},{8,10},{10,8},{12,... | collective-permute-start | bytes 1572872 | tf_op jit(solution)/shard_map/ppermute | solution.py:23
  228.6 24.5 %collective-permute-start.36 = (bf16[128,2048]{1,0:T(8,128)(2,1)S(1)}, bf16[128,2048]{1,0:T(8,128)(2,1)S(1)}, u32[]{:S(2)}, u32[]{:S(2)}) collective-permute-start(bf16[128,2048]{1,0:T(8,128)(2,1)S(1)} %fusion.5), channel_id=1, source_target_pairs={{0,24},{8,0},{16,8},{24,16},{1,25},{9,1},{17,9},{25,17},{2,26},{10... | collective-permute-start | bytes 1572872 | tf_op jit(solution)/shard_map/ppermute | solution.py:28
  229.4 24.9 %collective-permute-start.38 = (bf16[128,2048]{1,0:T(8,128)(2,1)S(1)}, bf16[128,2048]{1,0:T(8,128)(2,1)S(1)}, u32[]{:S(2)}, u32[]{:S(2)}) collective-permute-start(bf16[128,2048]{1,0:T(8,128)(2,1)S(1)} %fusion.6), channel_id=1, source_target_pairs={{0,8},{8,16},{16,24},{24,0},{1,9},{9,17},{17,25},{25,1},{2,10},{10... | collective-permute-start | bytes 1572872 | tf_op jit(solution)/shard_map/ppermute | solution.py:28
  253.5 9.2 %collective-permute-start.37 = (bf16[128,2048]{1,0:T(8,128)(2,1)S(1)}, bf16[128,2048]{1,0:T(8,128)(2,1)S(1)}, u32[]{:S(2)}, u32[]{:S(2)}) collective-permute-start(bf16[128,2048]{1,0:T(8,128)(2,1)S(1)} %add_convert_fusion.1), channel_id=1, source_target_pairs={{0,24},{8,0},{16,8},{24,16},{1,25},{9,1},{17,9},{25,17},{2,26},{10... | collective-permute-start | bytes 1572872 | tf_op jit(solution)/shard_map/ppermute | solution.py:28
